TPU v7x, 32 devices: a whole 2x2x4 slice. The times are simulated.
32 devices in a mesh: src: 16 (over z, x, core), tm: 2 (over y).
Axes of the slice: x: 2, y: 2, z: 4, core: 2. Of those that a mesh axis runs over, the one named last changes fastest.
Arguments:
- left_vector: float32 [2, 8192], P(None, ('src', 'tm')), may hold values from -12 to 12
- source_coeffs: float32 [5, 2, 8192], P(None, None, ('src', 'tm')), may hold values from -1.5 to 1.5
- knot_coeffs: float32 [12, 2, 8192], P(None, None, ('src', 'tm')), may hold values from -1.5 to 1.5
- source_index: int32 [2, 8192], P(None, ('src', 'tm')), may hold values from 0 to 1023
- band_start: int32 [2, 8192], P(None, ('src', 'tm')), may hold values from 0 to 1023, as said below
- bucket_fill: int32 [2, 32], P(None, ('src', 'tm')), may hold values from 51 to 256, as said below
- source_vector: float32 [5, 32768], P(None, ('src', 'tm')), may hold values from -6 to 6
- knot_vector: float32 [3, 2, 4096], P(None, 'tm', 'src'), may hold values from -6 to 6
- source_search: float32 [5, 32768], P(None, ('src', 'tm')), may hold values from -6 to 6
- knot_search: float32 [3, 2, 4096], P(None, 'tm', 'src'), may hold values from -6 to 6
- source_solution: float32 [5, 32768], P(None, ('src', 'tm')), may hold values from -6 to 6
- knot_solution: float32 [3, 2, 4096], P(None, 'tm', 'src'), may hold values from -6 to 6
- recurrence: float32 [3], replicated, may hold values from 0.5 to 1.5
Outputs:
- left_next: float32 [2, 8192], P(None, ('src', 'tm'))
- source_next: float32 [5, 32768], P(None, ('src', 'tm'))
- knot_next: float32 [3, 2, 4096], P(None, 'tm', 'src')
- search_source: float32 [5, 32768], P(None, ('src', 'tm'))
- search_knot: float32 [3, 2, 4096], P(None, 'tm', 'src')
- solution_source: float32 [5, 32768], P(None, ('src', 'tm'))
- solution_knot: float32 [3, 2, 4096], P(None, 'tm', 'src')
- recurrence_next: float32 [4], replicated
Inputs may be any that keep to these rules, and one draw needn't show every extreme that they name: `bucket_fill`: in every draw one bucket of some group block holds exactly 256 observations. Call band_start // 64 the knot owner of a slot. Among the 2 x 256 slots of one column block of 256, each knot owner is named at most 64 times, and in every block some owner exactly 64 times.
All inputs are finite; a program needn't handle non-finite values.
Results may differ from a plain program's by a relative error of at most 0.00002.
Values sent between devices are 32-bit elements; how exact they have to be, the bound alone decides.
No kernel may reach another device: no remote copies, remote signals or barrier semaphores. Data moves between devices by JAX's collectives and lax.ppermute only.
A program may use at most 64 MiB of HBM per device.

v0:
```python
import jax
import jax.numpy as jnp
from jax import lax
from jax.sharding import PartitionSpec as P

KB = 4
EPSILON = 1e-06


def band_positions(band_start, knots_slab):
    rows = jnp.arange(3 * KB, dtype=jnp.int32)
    base = rows // KB * knots_slab + rows % KB
    return base[:, None, None] + KB * band_start[None]


def shards(
    left_vector,
    source_coeffs,
    knot_coeffs,
    source_index,
    band_start,
    bucket_fill,
    source_vector,
    knot_vector,
    source_search,
    knot_search,
    source_solution,
    knot_solution,
    recurrence,
):
    slab_count = lax.axis_size("tm")
    group_count = lax.axis_size("src")
    devices = slab_count * group_count
    buckets, capacity = left_vector.shape
    source_dev = source_vector.shape[1]
    knot_dev = knot_vector.shape[2]
    knots_slab = knot_dev * group_count
    total_obs = buckets * capacity * devices
    unknowns = (5 * source_dev + 3 * knot_dev) * devices
    ratio = unknowns / total_obs
    alpha = recurrence[0]
    pivot = recurrence[1]
    remainder = recurrence[2]
    slot = lax.broadcasted_iota(jnp.int32, (buckets, capacity), 1)
    valid = (slot < bucket_fill).astype(jnp.float32)
    flat_source = source_index.reshape(-1)
    picked = jnp.take(source_vector, flat_source, axis=1).reshape(5, buckets, capacity)
    image = jnp.sum(source_coeffs * picked, axis=0)
    own_knots = knot_vector[:, 0, :]
    slab_whole = lax.all_gather(own_knots, "src", axis=1, tiled=True).reshape(-1)
    positions = band_positions(band_start, knots_slab)
    knot_image = jnp.sum(knot_coeffs * jnp.take(slab_whole, positions), axis=0)
    returned = lax.all_to_all(knot_image, "tm", split_axis=0, concat_axis=0, tiled=True)
    raw = valid * (image + returned - alpha * left_vector)
    own_squares = jnp.sum(raw * raw)
    arrived = lax.all_to_all(raw, "tm", split_axis=0, concat_axis=0, tiled=True)
    gradient_source = (
        jnp.zeros((5, source_dev), jnp.float32)
        .at[:, flat_source]
        .add((source_coeffs * raw[None]).reshape(5, -1))
    )
    knot_terms = (
        jnp.zeros((3 * knots_slab,), jnp.float32)
        .at[positions.reshape(-1)]
        .add((knot_coeffs * arrived[None]).reshape(-1))
        .reshape(3, knots_slab)
    )
    knot_totals = lax.psum(knot_terms, "src")
    gradient_knot = lax.dynamic_slice_in_dim(
        knot_totals, lax.axis_index("src") * knot_dev, knot_dev, 1
    )
    gradient_squares = jnp.sum(gradient_source * gradient_source) + jnp.sum(
        gradient_knot * gradient_knot
    )
    cross = jnp.sum(gradient_source * source_vector) + jnp.sum(gradient_knot * own_knots)
    old_squares = jnp.sum(source_vector * source_vector) + jnp.sum(own_knots * own_knots)
    norm_sums = lax.psum((own_squares, gradient_squares, cross, old_squares), ("src", "tm"))
    beta = jnp.sqrt(norm_sums[0] / total_obs + EPSILON)
    scaled = ratio / beta
    source_raw = scaled * gradient_source - beta * source_vector
    knot_raw = scaled * gradient_knot - beta * own_knots
    alpha_square = (
        scaled * scaled * norm_sums[1] - 2.0 * ratio * norm_sums[2] + beta * beta * norm_sums[3]
    )
    alpha_next = jnp.sqrt(alpha_square / unknowns + EPSILON)
    left_next = raw / beta
    source_next = source_raw / alpha_next
    knot_next = knot_raw / alpha_next
    radius = jnp.sqrt(pivot * pivot + beta * beta)
    cosine = pivot / radius
    sine = beta / radius
    coupling = sine * alpha_next
    step_gain = cosine * remainder
    solution_source = source_solution + step_gain / radius * source_search
    solution_knot = knot_solution + step_gain / radius * knot_search
    search_source = source_next - coupling / radius * source_search
    search_knot = knot_next[:, None, :] - coupling / radius * knot_search
    recurrence_next = jnp.stack([alpha_next, beta, -cosine * alpha_next, sine * remainder])
    return (
        left_next,
        source_next,
        knot_next[:, None, :],
        search_source,
        search_knot,
        solution_source,
        solution_knot,
        recurrence_next,
    )


def solution(mesh):
    in_specs = (
        P(None, ("src", "tm")),
        P(None, None, ("src", "tm")),
        P(None, None, ("src", "tm")),
        P(None, ("src", "tm")),
        P(None, ("src", "tm")),
        P(None, ("src", "tm")),
        P(None, ("src", "tm")),
        P(None, "tm", "src"),
        P(None, ("src", "tm")),
        P(None, "tm", "src"),
        P(None, ("src", "tm")),
        P(None, "tm", "src"),
        P(),
    )
    out_specs = (
        P(None, ("src", "tm")),
        P(None, ("src", "tm")),
        P(None, "tm", "src"),
        P(None, ("src", "tm")),
        P(None, "tm", "src"),
        P(None, ("src", "tm")),
        P(None, "tm", "src"),
        P(),
    )
    return jax.shard_map(shards, mesh=mesh, in_specs=in_specs, out_specs=out_specs, check_vma=False)
```

profile of v0, /device:TPU:14, one launch (start us, length us, event | category | flops | bytes accessed | tf_op | source)
XLA Modules:
  0.0 218.8 jit_solution(6217080422649008223)
XLA Ops:
  0.6 0.0 copy-start.11
  0.7 15.5 %all-gather = f32[3,1,4096]{2,1,0:T(1,128)S(1)} all-gather(f32[3,1,256]{2,1,0:T(1,128)} %param.20), channel_id=2, replica_groups=mesh['src'=16,'tm'=2] {'src'}, dimensions={2}, use_global_device_ids=true | all-gather | bytes 52224 | tf_op jit(solution)/shard_map/all_gather | solution.py:50
  16.1 0.0 copy-done.11
  16.2 0.1 fusion.3
  16.3 34.3 %gather_fusion.1 = f32[6144]{0:T(1024)S(1)} fusion(f32[12288]{0:T(1024)S(1)} %bitcast.51, s32[6144]{0:T(1024)S(1)} %broadcast_clamp_fusion), kind=kCustom, calls=%fused_computation.1 | custom fusion | bytes 73728 | tf_op jit(solution)/shard_map/jit(_take)/gather | solution.py:52
  50.6 0.0 copy-start.1
  50.6 0.7 copy-done.1
  51.3 0.0 copy-start
  51.3 0.1 fusion.6
  51.4 0.6 all_to_all.14
  52.0 3.7 %all-to-all-start = ((f32[2,1,256]{2,1,0:T(1,128)}), f32[2,1,256]{2,1,0:T(1,128)S(1)}, u32[]{:S(2)}, u32[]{:S(2)}) async-start(f32[2,1,256]{2,1,0:T(1,128)} %all_to_all.14), calls=%async_computation | async-start | bytes 4096 | tf_op jit(solution)/shard_map/all_to_all | solution.py:53
  55.7 0.1 broadcast_add_fusion
  55.8 0.0 copy-done
  55.8 0.2 copy.55
  56.0 0.0 copy-start.6
  56.1 0.7 multiply_reduce_fusion.2
  56.7 0.0 copy-done.6
  56.8 1.0 gather_fusion
  57.8 0.0 copy-start.7
  57.9 0.1 copy.56
  58.0 0.0 copy-start.2
  58.1 0.7 copy-done.2
  58.7 0.0 copy-done.7
  58.8 0.6 fusion.14
  60.6 0.0 all-to-all-done
  60.6 0.0 copy-start.10
  60.7 0.0 copy-start.12
  60.7 0.7 copy-done.10
  61.3 0.0 copy-done.12
  61.3 1.3 multiply_reduce_fusion.5
  62.7 0.1 copy.61
  62.8 0.6 copy.59
  63.4 3.3 %all-to-all-start.1 = ((f32[2,1,256]{2,1,0:T(1,128)}), f32[2,1,256]{2,1,0:T(1,128)S(1)}, u32[]{:S(2)}, u32[]{:S(2)}) async-start(f32[2,1,256]{2,1,0:T(1,128)} %copy.59), calls=%async_computation.1 | async-start | bytes 4096 | tf_op jit(solution)/shard_map/all_to_all | solution.py:56
  66.7 2.4 %scatter_custom_fusion = f32[5,1024]{0,1:T(8,128)S(1)} fusion(s32[512]{0:T(512)S(1)} %bitcast.59, f32[512,5]{1,0:T(8,128)S(1)} %bitcast.53, f32[]{:T(128)} %constant.77.clone.1), kind=kCustom, calls=%fused_computation.6 | custom fusion | flops 2560 | bytes 20484 | tf_op jit(solution)/shard_map/scatter-add | solution.py:60
  69.1 0.8 multiply_reduce_fusion
  69.8 0.2 copy.58
  70.0 0.0 all-to-all-done.1
  70.1 32.5 %scatter_custom_fusion.1 = f32[12288]{0:T(1024)S(1)} fusion(s32[6144]{0:T(1024)S(1)} %bitcast.56, f32[6144]{0:T(1024)S(1)} %bitcast.57, f32[]{:T(128)} %constant.77.clone.1), kind=kCustom, calls=%fused_computation.19 | custom fusion | flops 6144 | bytes 49156 | tf_op jit(solution)/shard_map/scatter-add | solution.py:65
  102.6 0.0 copy-start.8
  102.6 0.0 copy-start.9
  102.7 0.0 copy-start.5
  102.7 51.7 %psum.36 = f32[3,4096]{1,0:T(4,128)S(1)} all-reduce(f32[3,4096]{1,0:T(4,128)S(1)} %reshape.152), channel_id=1, replica_groups=mesh['src'=16,'tm'=2] {'src'}, use_global_device_ids=true, to_apply=%region_7.8 | all-reduce | flops 12288 | bytes 98304 | tf_op jit(solution)/shard_map/psum | solution.py:68
  154.4 0.0 copy-done.5
  154.4 0.6 fusion.9
  159.0 51.9 %all-reduce = (f32[]{:T(128)}, f32[]{:T(128)}, f32[]{:T(128)}, f32[]{:T(128)}) all-reduce(f32[]{:T(128)} %get-tuple-element.43, f32[]{:T(128)S(6)} %add.192, f32[]{:T(128)S(6)} %add.193, f32[]{:T(128)S(6)} %add.194), channel_id=1, replica_groups=mesh['src'=16,'tm'=2] {'src','tm'}, use_global_device_ids=true, to_apply=%region_3.4 | all-reduce | flops 4 | bytes 32 | tf_op jit(solution)/shard_map/psum | solution.py:77
  211.6 0.6 broadcast_divide_fusion
  214.2 0.0 copy-start.4
  214.9 0.0 copy-start.3
  216.3 0.6 broadcast_in_dim.37
  216.9 0.0 copy-done.8
  216.9 0.0 copy-done.9
  216.9 0.6 multiply_add_fusion.1
  217.5 0.0 copy-done.4
  217.5 0.0 copy-done.3
  217.5 0.6 multiply_subtract_fusion
  218.2 0.6 pad_maximum_fusion
  (18 shorter events, 0.2 us)
Async XLA Ops:
  0.6 15.5 %copy-start.11 = (s32[2,256]{1,0:T(2,128)S(1)}, s32[2,256]{1,0:T(2,128)}, u32[]{:S(2)}) copy-start(s32[2,256]{1,0:T(2,128)} %param.17) | copy-start | bytes 6148
  50.6 0.7 copy-start.1
  51.3 4.5 %copy-start = (f32[5,1024]{1,0:T(8,128)S(1)}, f32[5,1024]{1,0:T(8,128)}, u32[]{:S(2)}) copy-start(f32[5,1024]{1,0:T(8,128)} %param.19) | copy-start | bytes 61444
  52.0 8.6 %all-to-all-start = ((f32[2,1,256]{2,1,0:T(1,128)}), f32[2,1,256]{2,1,0:T(1,128)S(1)}, u32[]{:S(2)}, u32[]{:S(2)}) async-start(f32[2,1,256]{2,1,0:T(1,128)} %all_to_all.14), calls=%async_computation | async-start | bytes 4096 | tf_op jit(solution)/shard_map/all_to_all | solution.py:53
  56.0 0.7 copy-start.6
  57.8 0.9 copy-start.7
  58.0 0.7 copy-start.2
  60.6 0.7 copy-start.10
  60.7 0.7 copy-start.12
  63.4 6.6 %all-to-all-start.1 = ((f32[2,1,256]{2,1,0:T(1,128)}), f32[2,1,256]{2,1,0:T(1,128)S(1)}, u32[]{:S(2)}, u32[]{:S(2)}) async-start(f32[2,1,256]{2,1,0:T(1,128)} %copy.59), calls=%async_computation.1 | async-start | bytes 4096 | tf_op jit(solution)/shard_map/all_to_all | solution.py:56
  102.6 114.3 %copy-start.8 = (f32[3,1,256]{2,1,0:T(1,128)S(1)}, f32[3,1,256]{2,1,0:T(1,128)}, u32[]{:S(2)}) copy-start(f32[3,1,256]{2,1,0:T(1,128)} %param.24) | copy-start | bytes 9220
  102.6 114.3 %copy-start.9 = (f32[3,1,256]{2,1,0:T(1,128)S(1)}, f32[3,1,256]{2,1,0:T(1,128)}, u32[]{:S(2)}) copy-start(f32[3,1,256]{2,1,0:T(1,128)} %param.22) | copy-start | bytes 9220
  102.7 51.8 %copy-start.5 = (f32[3,1,256]{2,1,0:T(1,128)S(1)}, f32[3,1,256]{2,1,0:T(1,128)}, u32[]{:S(2)}) copy-start(f32[3,1,256]{2,1,0:T(1,128)} %param.20) | copy-start | bytes 9220
  214.2 3.3 %copy-start.4 = (f32[5,1024]{1,0:T(8,128)S(1)}, f32[5,1024]{1,0:T(8,128)}, u32[]{:S(2)}) copy-start(f32[5,1024]{1,0:T(8,128)} %param.23) | copy-start | bytes 61444
  214.9 2.6 %copy-start.3 = (f32[5,1024]{1,0:T(8,128)S(1)}, f32[5,1024]{1,0:T(8,128)}, u32[]{:S(2)}) copy-start(f32[5,1024]{1,0:T(8,128)} %param.21) | copy-start | bytes 61444
where the time goes:
time: 220 us; the launch traced here: 219 us
  blocking collectives  119 us (54%)
  other arithmetic  41.1 us (19%)
  local copies, waits for them, and re-layouts  40.5 us (18%)
  between operations  11 us (5%)
  starting transfers between devices  7 us (3%)
    psum x1, blocking collectives, shards(): lax.psum((own_squares, gradient_squares, cross, old_squares), ('src', 'tm'))  51.9 us
    psum x1, blocking collectives, shards(): knot_totals = lax.psum(knot_terms, 'src')  51.7 us
    gather x2, local copies, waits for them, and re-layouts, shards(): knot_image = jnp.sum(knot_coeffs * jnp.take(slab_whole, positions), axis=0)  34.3 us
    scatter-add x1, other arithmetic, shards(): knot_terms = jnp.zeros((3 * knots_slab,), jnp.float32).at[positions.resha...  32.5 us
    all_gather x1, blocking collectives, shards(): lax.all_gather(own_knots, 'src', axis=1, tiled=True).reshape(-1)  15.5 us
  transfers between devices with their start and end apart: 2, of which 0 were waited for; matrix products, arithmetic and copies ran while one was open for 3% of the time, Pallas kernels for 0%

commit v1 on v0

--- a/solution.py
+++ b/solution.py
@@ -65,7 +65,11 @@
         .add((knot_coeffs * arrived[None]).reshape(-1))
         .reshape(3, knots_slab)
     )
-    knot_totals = lax.psum(knot_terms, "src")
+    knot_totals = knot_terms
+    for hop in (1, 2, 4, 8):
+        knot_totals = knot_totals + lax.ppermute(
+            knot_totals, "src", [(dev, dev ^ hop) for dev in range(16)]
+        )
     gradient_knot = lax.dynamic_slice_in_dim(
         knot_totals, lax.axis_index("src") * knot_dev, knot_dev, 1
     )

time: 220 us -> 176 us (0.80)
  blocking collectives: 119 us -> 58.1 us
  starting transfers between devices: 7 us -> 15.3 us
  waiting for transfers between devices: 0.01 us -> 7.64 us
    psum x1 -> x0, blocking collectives: 51.7 us -> none  [shards(): knot_totals = lax.psum(knot_terms, 'src')]
    psum x1, blocking collectives: 51.9 us -> 42.6 us  [shards(): lax.psum((own_squares, gradient_squares, cross, old_squares), ('src', 'tm'))]
    ppermute x0 -> x4, starting transfers between devices: none -> 7.8 us  [shards(): lax.ppermute(knot_totals, 'src', [(dev, dev ^ hop) for dev in range(16)])]
    ppermute x0 -> x4, waiting for transfers between devices: none -> 5.9 us  [shards(): lax.ppermute(knot_totals, 'src', [(dev, dev ^ hop) for dev in range(16)])]
  transfers between devices with their start and end apart: 2 -> 6, of which waited for: 0 -> 4; matrix products, arithmetic and copies ran while one was open for 3% -> 4% of each run, Pallas kernels for 0% -> 0%
where the time goes in v1:
time: 176 us; the launch traced here: 174 us
  blocking collectives  58.1 us (33%)
  other arithmetic  41.1 us (23%)
  local copies, waits for them, and re-layouts  40.9 us (23%)
  starting transfers between devices  15.3 us (9%)
  between operations  11 us (6%)
  waiting for transfers between devices  7.64 us (4%)
    psum x1, blocking collectives, shards(): lax.psum((own_squares, gradient_squares, cross, old_squares), ('src', 'tm'))  42.6 us
    gather x2, local copies, waits for them, and re-layouts, shards(): knot_image = jnp.sum(knot_coeffs * jnp.take(slab_whole, positions), axis=0)  34.3 us
    scatter-add x1, other arithmetic, shards(): knot_terms = jnp.zeros((3 * knots_slab,), jnp.float32).at[positions.resha...  32.5 us
    all_gather x1, blocking collectives, shards(): lax.all_gather(own_knots, 'src', axis=1, tiled=True).reshape(-1)  15.5 us
    ppermute x4, starting transfers between devices, shards(): lax.ppermute(knot_totals, 'src', [(dev, dev ^ hop) for dev in range(16)])  7.8 us
    ppermute x4, waiting for transfers between devices, shards(): lax.ppermute(knot_totals, 'src', [(dev, dev ^ hop) for dev in range(16)])  5.9 us
    all_to_all x1, starting transfers between devices, shards(): arrived = lax.all_to_all(raw, 'tm', split_axis=0, concat_axis=0, tiled=True)  3.75 us
    all_to_all x1, starting transfers between devices, shards(): lax.all_to_all(knot_image, 'tm', split_axis=0, concat_axis=0, tiled=True)  3.71 us
  transfers between devices with their start and end apart: 6, of which 4 were waited for; matrix products, arithmetic and copies ran while one was open for 4% of the time, Pallas kernels for 0%

profile of v1, /device:TPU:14, one launch (start us, length us, event | category | flops | bytes accessed | tf_op | source)
XLA Modules:
  0.0 174.0 jit_solution(16106959279230489342)
XLA Ops:
  0.6 0.0 copy-start.11
  0.7 15.5 %all-gather = f32[3,1,4096]{2,1,0:T(1,128)S(1)} all-gather(f32[3,1,256]{2,1,0:T(1,128)} %param.20), channel_id=2, replica_groups=mesh['src'=16,'tm'=2] {'src'}, dimensions={2}, use_global_device_ids=true | all-gather | bytes 52224 | tf_op jit(solution)/shard_map/all_gather | solution.py:50
  16.1 0.0 copy-done.11
  16.2 0.1 fusion.3
  16.3 34.3 %gather_fusion.1 = f32[6144]{0:T(1024)S(1)} fusion(f32[12288]{0:T(1024)S(1)} %bitcast.51, s32[6144]{0:T(1024)S(1)} %broadcast_clamp_fusion), kind=kCustom, calls=%fused_computation.1 | custom fusion | bytes 73728 | tf_op jit(solution)/shard_map/jit(_take)/gather | solution.py:52
  50.6 0.0 copy-start.1
  50.6 0.7 copy-done.1
  51.3 0.0 copy-start
  51.3 0.1 fusion.6
  51.4 0.6 all_to_all.14
  52.0 3.7 %all-to-all-start = ((f32[2,1,256]{2,1,0:T(1,128)}), f32[2,1,256]{2,1,0:T(1,128)S(1)}, u32[]{:S(2)}, u32[]{:S(2)}) async-start(f32[2,1,256]{2,1,0:T(1,128)} %all_to_all.14), calls=%async_computation | async-start | bytes 4096 | tf_op jit(solution)/shard_map/all_to_all | solution.py:53
  55.7 0.1 broadcast_add_fusion
  55.8 0.0 copy-done
  55.8 0.0 copy-start.6
  55.8 0.2 copy.55
  56.1 0.4 copy-done.6
  56.5 1.0 gather_fusion
  57.6 0.0 copy-start.2
  57.6 0.0 copy-start.7
  57.6 0.1 copy.56
  57.7 0.6 copy-done.2
  58.3 0.0 copy-done.7
  58.3 0.6 fusion.14
  58.9 0.0 all-to-all-done
  59.0 0.0 copy-start.10
  59.0 0.0 copy-start.12
  59.0 0.7 copy-done.10
  59.6 0.0 copy-done.12
  59.6 1.3 multiply_reduce_fusion.5
  61.0 0.6 copy.59
  61.5 3.8 %all-to-all-start.1 = ((f32[2,1,256]{2,1,0:T(1,128)}), f32[2,1,256]{2,1,0:T(1,128)S(1)}, u32[]{:S(2)}, u32[]{:S(2)}) async-start(f32[2,1,256]{2,1,0:T(1,128)} %copy.59), calls=%async_computation.1 | async-start | bytes 4096 | tf_op jit(solution)/shard_map/all_to_all | solution.py:56
  65.3 1.7 all-to-all-done.1
  67.1 32.5 %scatter_custom_fusion.1 = f32[12288]{0:T(1024)S(1)} fusion(s32[6144]{0:T(1024)S(1)} %bitcast.56, f32[6144]{0:T(1024)S(1)} %bitcast.57, f32[]{:T(128)} %constant.77.clone.1), kind=kCustom, calls=%fused_computation.19 | custom fusion | flops 6144 | bytes 49156 | tf_op jit(solution)/shard_map/scatter-add | solution.py:65
  99.7 0.1 collective-permute-start
  99.8 1.2 collective-permute-done
  101.0 4.3 %collective-permute-start.1 = (f32[3,4096]{1,0:T(4,128)S(1)}, f32[3,4096]{1,0:T(4,128)S(1)}, u32[]{:S(2)}, u32[]{:S(2)}) collective-permute-start(f32[3,4096]{1,0:T(4,128)S(1)} %add.201), channel_id=1, source_target_pairs={{0,4},{2,6},{4,0},{6,2},{8,12},{10,14},{12,8},{14,10},{16,20},{18,... | collective-permute-start | bytes 147464 | tf_op jit(solution)/shard_map/ppermute | solution.py:70
  105.3 0.7 multiply_reduce_fusion.2
  107.3 0.4 collective-permute-done.1
  107.8 3.3 %collective-permute-start.2 = (f32[3,4096]{1,0:T(4,128)S(1)}, f32[3,4096]{1,0:T(4,128)S(1)}, u32[]{:S(2)}, u32[]{:S(2)}) collective-permute-start(f32[3,4096]{1,0:T(4,128)S(1)} %add.202), channel_id=1, source_target_pairs={{0,8},{2,10},{4,12},{6,14},{8,0},{10,2},{12,4},{14,6},{16,24},{18,... | collective-permute-start | bytes 147464 | tf_op jit(solution)/shard_map/ppermute | solution.py:70
  111.1 0.1 copy.61
  111.3 2.4 %scatter_custom_fusion = f32[5,1024]{0,1:T(8,128)S(1)} fusion(s32[512]{0:T(512)S(1)} %bitcast.59, f32[512,5]{1,0:T(8,128)S(1)} %bitcast.53, f32[]{:T(128)} %constant.77.clone.1), kind=kCustom, calls=%fused_computation.6 | custom fusion | flops 2560 | bytes 20484 | tf_op jit(solution)/shard_map/scatter-add | solution.py:60
  113.6 0.0 collective-permute-done.2
  113.7 0.1 collective-permute-start.3
  113.8 0.8 multiply_reduce_fusion
  114.5 0.0 copy-start.5
  114.5 0.0 copy-start.8
  114.6 0.0 copy-start.9
  114.6 0.2 copy.58
  114.7 4.2 %collective-permute-done.3 = f32[3,4096]{1,0:T(4,128)S(1)} collective-permute-done((f32[3,4096]{1,0:T(4,128)S(1)}, f32[3,4096]{1,0:T(4,128)S(1)}, u32[]{:S(2)}, u32[]{:S(2)}) %collective-permute-start.3) | collective-permute-done | bytes 49184 | tf_op jit(solution)/shard_map/ppermute | solution.py:70
  119.0 0.0 copy-done.5
  119.0 0.6 fusion.9
  123.5 42.6 %all-reduce = (f32[]{:T(128)}, f32[]{:T(128)}, f32[]{:T(128)}, f32[]{:T(128)}) all-reduce(f32[]{:T(128)} %get-tuple-element.44, f32[]{:T(128)S(6)} %add.206, f32[]{:T(128)S(6)} %add.207, f32[]{:T(128)S(6)} %add.208), channel_id=1, replica_groups=mesh['src'=16,'tm'=2] {'src','tm'}, use_global_device_ids=true, to_apply=%region_3.4 | all-reduce | flops 4 | bytes 32 | tf_op jit(solution)/shard_map/psum | solution.py:81
  166.8 0.6 broadcast_divide_fusion
  170.1 0.0 copy-start.3
  170.1 0.0 copy-start.4
  171.6 0.6 broadcast_in_dim.37
  172.1 0.0 copy-done.8
  172.1 0.0 copy-done.9
  172.1 0.6 multiply_add_fusion.1
  172.7 0.0 copy-done.3
  172.7 0.0 copy-done.4
  172.7 0.6 multiply_subtract_fusion
  173.4 0.6 pad_maximum_fusion
  (21 shorter events, 0.3 us)
Async XLA Ops:
  0.6 15.5 %copy-start.11 = (s32[2,256]{1,0:T(2,128)S(1)}, s32[2,256]{1,0:T(2,128)}, u32[]{:S(2)}) copy-start(s32[2,256]{1,0:T(2,128)} %param.17) | copy-start | bytes 6148
  50.6 0.7 copy-start.1
  51.3 4.5 %copy-start = (f32[5,1024]{1,0:T(8,128)S(1)}, f32[5,1024]{1,0:T(8,128)}, u32[]{:S(2)}) copy-start(f32[5,1024]{1,0:T(8,128)} %param.19) | copy-start | bytes 61444
  52.0 6.9 %all-to-all-start = ((f32[2,1,256]{2,1,0:T(1,128)}), f32[2,1,256]{2,1,0:T(1,128)S(1)}, u32[]{:S(2)}, u32[]{:S(2)}) async-start(f32[2,1,256]{2,1,0:T(1,128)} %all_to_all.14), calls=%async_computation | async-start | bytes 4096 | tf_op jit(solution)/shard_map/all_to_all | solution.py:53
  55.8 0.7 copy-start.6
  57.6 0.7 copy-start.2
  57.6 0.7 copy-start.7
  59.0 0.7 copy-start.10
  59.0 0.7 copy-start.12
  61.5 5.5 %all-to-all-start.1 = ((f32[2,1,256]{2,1,0:T(1,128)}), f32[2,1,256]{2,1,0:T(1,128)S(1)}, u32[]{:S(2)}, u32[]{:S(2)}) async-start(f32[2,1,256]{2,1,0:T(1,128)} %copy.59), calls=%async_computation.1 | async-start | bytes 4096 | tf_op jit(solution)/shard_map/all_to_all | solution.py:56
  99.7 1.3 collective-permute-start
  101.0 6.7 %collective-permute-start.1 = (f32[3,4096]{1,0:T(4,128)S(1)}, f32[3,4096]{1,0:T(4,128)S(1)}, u32[]{:S(2)}, u32[]{:S(2)}) collective-permute-start(f32[3,4096]{1,0:T(4,128)S(1)} %add.201), channel_id=1, source_target_pairs={{0,4},{2,6},{4,0},{6,2},{8,12},{10,14},{12,8},{14,10},{16,20},{18,... | collective-permute-start | bytes 147464 | tf_op jit(solution)/shard_map/ppermute | solution.py:70
  107.8 5.9 %collective-permute-start.2 = (f32[3,4096]{1,0:T(4,128)S(1)}, f32[3,4096]{1,0:T(4,128)S(1)}, u32[]{:S(2)}, u32[]{:S(2)}) collective-permute-start(f32[3,4096]{1,0:T(4,128)S(1)} %add.202), channel_id=1, source_target_pairs={{0,8},{2,10},{4,12},{6,14},{8,0},{10,2},{12,4},{14,6},{16,24},{18,... | collective-permute-start | bytes 147464 | tf_op jit(solution)/shard_map/ppermute | solution.py:70
  113.7 5.3 %collective-permute-start.3 = (f32[3,4096]{1,0:T(4,128)S(1)}, f32[3,4096]{1,0:T(4,128)S(1)}, u32[]{:S(2)}, u32[]{:S(2)}) collective-permute-start(f32[3,4096]{1,0:T(4,128)S(1)} %add.203), channel_id=1, source_target_pairs={{0,16},{2,18},{4,20},{6,22},{8,24},{10,26},{12,28},{14,30},{16,0},... | collective-permute-start | bytes 147464 | tf_op jit(solution)/shard_map/ppermute | solution.py:70
  114.5 4.4 %copy-start.5 = (f32[3,1,256]{2,1,0:T(1,128)S(1)}, f32[3,1,256]{2,1,0:T(1,128)}, u32[]{:S(2)}) copy-start(f32[3,1,256]{2,1,0:T(1,128)} %param.20) | copy-start | bytes 9220
  114.5 57.6 %copy-start.8 = (f32[3,1,256]{2,1,0:T(1,128)S(1)}, f32[3,1,256]{2,1,0:T(1,128)}, u32[]{:S(2)}) copy-start(f32[3,1,256]{2,1,0:T(1,128)} %param.24) | copy-start | bytes 9220
  114.6 57.6 %copy-start.9 = (f32[3,1,256]{2,1,0:T(1,128)S(1)}, f32[3,1,256]{2,1,0:T(1,128)}, u32[]{:S(2)}) copy-start(f32[3,1,256]{2,1,0:T(1,128)} %param.22) | copy-start | bytes 9220
  170.1 2.6 %copy-start.3 = (f32[5,1024]{1,0:T(8,128)S(1)}, f32[5,1024]{1,0:T(8,128)}, u32[]{:S(2)}) copy-start(f32[5,1024]{1,0:T(8,128)} %param.21) | copy-start | bytes 61444
  170.1 2.6 %copy-start.4 = (f32[5,1024]{1,0:T(8,128)S(1)}, f32[5,1024]{1,0:T(8,128)}, u32[]{:S(2)}) copy-start(f32[5,1024]{1,0:T(8,128)} %param.23) | copy-start | bytes 61444
